TPU v7x, 32 devices: a whole 2x2x4 slice. The times are simulated.
32 devices in a mesh: group: 2 (over x), tensor: 16 (over z, y, core).
Axes of the slice: x: 2, y: 2, z: 4, core: 2. Of those that a mesh axis runs over, the one named last changes fastest.
Arguments:
- residual_input: bfloat16 [32, 8192], P('group', 'tensor'), parts along dimension 0, may hold values from -40 to 40
- attention_norm_gain: bfloat16 [8192], replicated, may hold values from 0.3984375 to 2.5
- query_weight: bfloat16 [8192, 8192], P(None, 'tensor'), may hold values from -0.0625 to 0.0625
- key_value_weight: bfloat16 [8192, 2048], P(None, 'tensor'), may hold values from -0.0625 to 0.0625
- output_weight: bfloat16 [8192, 8192], P('tensor'), may hold values from -0.09375 to 0.09375
- adapter_down_weight: bfloat16 [16, 8192, 192], P('group', 'tensor'), parts along dimension 0, may hold values from -0.0625 to 0.0625
- adapter_up_query: bfloat16 [16, 64, 8192], P('group', None, 'tensor'), parts along dimension 0, may hold values from -0.75 to 0.75
- adapter_up_key_value: bfloat16 [16, 64, 2048], P('group', None, 'tensor'), parts along dimension 0, may hold values from -0.75 to 0.75
- stored_key_cache: bfloat16 [32, 512, 1024], P(('group', 'tensor')), parts along dimension 0, may hold values from -250 to 250
- stored_value_cache: bfloat16 [32, 512, 1024], P(('group', 'tensor')), parts along dimension 0, may hold values from -8 to 8
- row_adapter_index: int32 [32], P('group'), parts along dimension 0, may hold values from 0 to 7
- cache_live_length: int32 [32], P(('group', 'tensor')), parts along dimension 0, may hold values from 2 to 508, as said below
Outputs:
- hidden_out: bfloat16 [32, 8192], P('group', 'tensor'), parts along dimension 0
- new_keyval: bfloat16 [32, 4, 2048], P(('group', 'tensor')), parts along dimension 0
There are 2 independent parts, one for each index of `group`. A program takes and returns all parts, laid end to end along the dimension named above; an argument that names none is the same for every part. Nothing has to cross between parts.
Inputs may be any that keep to these rules, and one draw needn't show every extreme that they name: `cache_live_length`: some row's length is exactly 508, so every new key fits the cache.
All inputs are finite; a program needn't handle non-finite values.
Results may differ from a plain program's by a relative error of at most 0.029.
The roundings to bfloat16 on the way count: a program that leaves them out, or rounds other values in their place, can miss the bound.
Values may be sent and summed in bfloat16 or wider, within the bound.
A program may use at most 128 MiB of HBM per device.

v0:
```python
import jax
import jax.numpy as jnp
from jax import lax
from jax.sharding import PartitionSpec as P

QUERY_HEADS = 64
KEY_VALUE_HEADS = 8
HEAD_SIZE = 128
ADAPTER_RANK = 64
ADAPTER_COUNT = 8
BLK = 16
CACHE_CAPACITY = 512
DECODE_STEPS = 4


eps = 1e-05
rope_base = 500000.0
adapter_scale = 0.5


def apply_rotary(values_in, token_positions):
    halfway = HEAD_SIZE // 2
    frequency = rope_base ** (-jnp.arange(halfway, dtype=jnp.float32) / halfway)
    angles = token_positions.astype(jnp.float32)[:, None] * frequency[None, :]
    cosine = jnp.cos(angles)[:, None, :]
    sine_part = jnp.sin(angles)[:, None, :]
    first_half = values_in[..., :halfway]
    second_half = values_in[..., halfway:]
    return jnp.concatenate(
        [
            first_half * cosine - second_half * sine_part,
            second_half * cosine + first_half * sine_part,
        ],
        axis=-1,
    )


def rms_norm(hidden_state, gain_vec):
    widened = hidden_state.astype(jnp.float32)
    mean_sq = jnp.mean(widened * widened, axis=1, keepdims=True)
    return (widened * lax.rsqrt(mean_sq + eps) * gain_vec.astype(jnp.float32)[None, :]).astype(
        jnp.bfloat16
    )


def block_tables(row_adapter_index):
    total_row_count = row_adapter_index.shape[0]
    nblocks = total_row_count // BLK + ADAPTER_COUNT
    onehot = (
        row_adapter_index[:, None] == jnp.arange(ADAPTER_COUNT, dtype=jnp.int32)[None, :]
    ).astype(jnp.int32)
    counts = jnp.sum(onehot, axis=0)
    adapter_partial = (counts + BLK - 1) // BLK
    first_block = jnp.cumsum(adapter_partial) - adapter_partial
    earlier = jnp.cumsum(onehot, axis=0) - onehot
    rank_in = jnp.sum(onehot * earlier, axis=1)
    start_block = jnp.sum(onehot * first_block[None, :], axis=1)
    slot_of_row = (start_block + rank_in // BLK) * BLK + rank_in % BLK
    slots = jnp.arange(nblocks * BLK, dtype=jnp.int32)
    matches = (slot_of_row[None, :] == slots[:, None]).astype(jnp.int32)
    filled = jnp.sum(matches, axis=1)
    row_of_slot = jnp.sum(matches * jnp.arange(total_row_count, dtype=jnp.int32)[None, :], axis=1)
    blocks = jnp.arange(nblocks, dtype=jnp.int32)
    block_end = first_block + adapter_partial
    owner = jnp.minimum(
        jnp.sum((block_end[None, :] <= blocks[:, None]).astype(jnp.int32), axis=1),
        ADAPTER_COUNT - 1,
    )
    return (slot_of_row, row_of_slot, filled, owner)


def split_into_blocks(inputs, weights, page_tables):
    slot_of_row, row_of_slot, filled, owner = page_tables
    nblocks = owner.shape[0]
    gathered = jnp.take(inputs, row_of_slot, axis=0) * filled[:, None].astype(inputs.dtype)
    gathered = gathered.reshape(nblocks, BLK, inputs.shape[1])
    chosen = jnp.take(weights, owner, axis=0)
    products = jnp.einsum("bsk,bkm->bsm", gathered, chosen, preferred_element_type=jnp.float32)
    return jnp.take(products.reshape(nblocks * BLK, weights.shape[2]), slot_of_row, axis=0)


def attend(
    query_projected,
    key_value_proj,
    stored_key_cache,
    stored_value_cache,
    cache_live_length,
    newest_keys,
    newest_values,
    single_decode_pass,
):
    moved_query, shifted_key_value = (
        lax.all_to_all(query_projected, "tensor", split_axis=0, concat_axis=1, tiled=True),
        lax.all_to_all(key_value_proj, "tensor", split_axis=0, concat_axis=1, tiled=True),
    )
    replica_local_count = moved_query.shape[0]
    query_group_count = QUERY_HEADS // KEY_VALUE_HEADS
    key_value_width = KEY_VALUE_HEADS * HEAD_SIZE
    token_positions = cache_live_length + single_decode_pass
    rotated_query_rows = apply_rotary(
        moved_query.astype(jnp.float32).reshape(replica_local_count, QUERY_HEADS, HEAD_SIZE),
        token_positions,
    ).astype(jnp.bfloat16)
    rotated_key_rows = apply_rotary(
        shifted_key_value[:, :key_value_width]
        .astype(jnp.float32)
        .reshape(replica_local_count, KEY_VALUE_HEADS, HEAD_SIZE),
        token_positions,
    ).astype(jnp.bfloat16)
    newest_keys = newest_keys.at[:, single_decode_pass].set(rotated_key_rows)
    newest_values = newest_values.at[:, single_decode_pass].set(
        shifted_key_value[:, key_value_width:].reshape(
            replica_local_count, KEY_VALUE_HEADS, HEAD_SIZE
        )
    )
    grouped_query = rotated_query_rows.reshape(
        replica_local_count, KEY_VALUE_HEADS, query_group_count, HEAD_SIZE
    )
    previous_keys = stored_key_cache.reshape(
        replica_local_count, CACHE_CAPACITY, KEY_VALUE_HEADS, HEAD_SIZE
    )
    previous_values = stored_value_cache.reshape(
        replica_local_count, CACHE_CAPACITY, KEY_VALUE_HEADS, HEAD_SIZE
    )
    old_scores = jnp.einsum(
        "rkgd,rjkd->rkgj", grouped_query, previous_keys, preferred_element_type=jnp.float32
    ) * HEAD_SIZE ** (-0.5)
    live_mask = jnp.arange(CACHE_CAPACITY, dtype=jnp.int32)[None, :] < cache_live_length[:, None]
    old_scores = jnp.where(live_mask[:, None, None, :], old_scores, -jnp.inf)
    new_scores = jnp.einsum(
        "rkgd,rmkd->rkgm", grouped_query, newest_keys, preferred_element_type=jnp.float32
    ) * HEAD_SIZE ** (-0.5)
    visible = jnp.arange(DECODE_STEPS, dtype=jnp.int32)[None, None, None, :] <= single_decode_pass
    new_scores = jnp.where(visible, new_scores, -jnp.inf)
    row_top = jnp.maximum(
        jnp.max(old_scores, axis=3, keepdims=True), jnp.max(new_scores, axis=3, keepdims=True)
    )
    old_exp = jnp.exp(old_scores - row_top)
    new_exp = jnp.exp(new_scores - row_top)
    denominator = jnp.sum(old_exp, axis=3, keepdims=True) + jnp.sum(new_exp, axis=3, keepdims=True)
    old_weights = (old_exp / denominator).astype(jnp.bfloat16)
    new_weights = (new_exp / denominator).astype(jnp.bfloat16)
    mixture = jnp.einsum(
        "rkgj,rjkd->rkgd", old_weights, previous_values, preferred_element_type=jnp.float32
    )
    mixture = mixture + jnp.einsum(
        "rkgm,rmkd->rkgd", new_weights, newest_values, preferred_element_type=jnp.float32
    )
    attended_rows = mixture.astype(jnp.bfloat16).reshape(
        replica_local_count, QUERY_HEADS * HEAD_SIZE
    )
    return (attended_rows, newest_keys, newest_values)


def body(
    residual_input,
    attention_norm_gain,
    query_weight,
    key_value_weight,
    output_weight,
    adapter_down_weight,
    adapter_up_query,
    adapter_up_key_value,
    stored_key_cache,
    stored_value_cache,
    row_adapter_index,
    cache_live_length,
):
    devices_along = lax.axis_size("tensor")
    position_in = lax.axis_index("tensor")
    share_width = residual_input.shape[1]
    replica_local_count = stored_key_cache.shape[0]
    key_value_width = KEY_VALUE_HEADS * HEAD_SIZE
    page_tables = block_tables(row_adapter_index)
    newest_keys = jnp.zeros(
        (replica_local_count, DECODE_STEPS, KEY_VALUE_HEADS, HEAD_SIZE), jnp.bfloat16
    )
    newest_values = jnp.zeros(
        (replica_local_count, DECODE_STEPS, KEY_VALUE_HEADS, HEAD_SIZE), jnp.bfloat16
    )
    hidden_state = residual_input
    for single_decode_pass in range(DECODE_STEPS):
        gathered = lax.all_gather(hidden_state, "tensor", axis=1, tiled=True)
        normalized_input = rms_norm(gathered, attention_norm_gain)
        normalized_portion = lax.dynamic_slice_in_dim(
            normalized_input, position_in * share_width, share_width, 1
        )
        reduced_features = lax.psum(
            split_into_blocks(normalized_portion, adapter_down_weight, page_tables), "tensor"
        ).astype(jnp.bfloat16)
        query_projected = jnp.dot(
            normalized_input, query_weight, preferred_element_type=jnp.float32
        )
        query_projected = query_projected + adapter_scale * split_into_blocks(
            reduced_features[:, :ADAPTER_RANK], adapter_up_query, page_tables
        )
        selected_rank = jnp.where(
            position_in < devices_along // 2,
            reduced_features[:, ADAPTER_RANK : 2 * ADAPTER_RANK],
            reduced_features[:, 2 * ADAPTER_RANK :],
        )
        key_value_proj = jnp.dot(
            normalized_input, key_value_weight, preferred_element_type=jnp.float32
        )
        key_value_proj = key_value_proj + adapter_scale * split_into_blocks(
            selected_rank, adapter_up_key_value, page_tables
        )
        attended_rows, newest_keys, newest_values = attend(
            query_projected.astype(jnp.bfloat16),
            key_value_proj.astype(jnp.bfloat16),
            stored_key_cache,
            stored_value_cache,
            cache_live_length,
            newest_keys,
            newest_values,
            single_decode_pass,
        )
        attended = lax.all_to_all(attended_rows, "tensor", split_axis=1, concat_axis=0, tiled=True)
        out_term = jnp.dot(attended, output_weight, preferred_element_type=jnp.float32)
        summed = lax.psum_scatter(out_term, "tensor", scatter_dimension=1, tiled=True)
        hidden_state = (hidden_state.astype(jnp.float32) + summed).astype(jnp.bfloat16)
    new_keyval = jnp.concatenate(
        [
            newest_keys.reshape(replica_local_count, DECODE_STEPS, key_value_width),
            newest_values.reshape(replica_local_count, DECODE_STEPS, key_value_width),
        ],
        axis=2,
    )
    return (hidden_state, new_keyval)


def solution(mesh):
    in_specs = (
        P("group", "tensor"),
        P(),
        P(None, "tensor"),
        P(None, "tensor"),
        P("tensor", None),
        P("group", "tensor", None),
        P("group", None, "tensor"),
        P("group", None, "tensor"),
        P(("group", "tensor"), None, None),
        P(("group", "tensor"), None, None),
        P("group"),
        P(("group", "tensor")),
    )
    out_specs = (P("group", "tensor"), P(("group", "tensor"), None, None))
    return jax.shard_map(body, mesh=mesh, in_specs=in_specs, out_specs=out_specs, check_vma=False)
```

profile of v0, /device:TPU:0, one launch (start us, length us, event | category | flops | bytes accessed | tf_op | source)
XLA Modules:
  0.0 781.9 jit_solution(3729545610740416735)
XLA Ops:
  10.8 24.0 %all_gather.12 = bf16[16,8192]{1,0:T(8,128)(2,1)S(1)} all-gather(bf16[16,512]{1,0:T(8,128)(2,1)} %param.44), channel_id=1, replica_groups=mesh['group'=2,'tensor'=16] {'tensor'}, dimensions={1}, use_global_device_ids=true | all-gather | bytes 278528 | tf_op jit(solution)/shard_map/all_gather | solution.py:183
  36.2 3.4 gather_fusion.1
  39.6 1.7 broadcast_select_fusion
  43.8 57.8 %psum.28 = bf16[16,192]{1,0:T(8,128)(2,1)S(1)} all-reduce(f32[16,192]{1,0:T(8,128)S(1)} %broadcast_select_fusion.6), channel_id=1, replica_groups=mesh['group'=2,'tensor'=16] {'tensor'}, use_global_device_ids=true, to_apply=%region_9.13 | all-reduce | flops 3072 | bytes 18432 | tf_op jit(solution)/shard_map/psum | solution.py:188
  105.7 3.5 all-to-all-start.1
  112.4 4.6 fusion.15
  120.2 2.5 copy.143
  122.7 6.0 all-to-all-start
  128.8 6.3 all-to-all-done
  138.7 9.1 %all_to_all.184 = bf16[16,2,256]{2,1,0:T(2,128)(2,1)S(1)} all-to-all(bf16[16,2,256]{2,1,0:T(2,128)(2,1)S(1)} %reshape.1749), channel_id=1, replica_groups=mesh['group'=2,'tensor'=16] {'tensor'}, dimensions={0} | all-to-all | bytes 32768 | tf_op jit(solution)/shard_map/all_to_all | solution.py:218
  147.8 5.4 fusion.83
  155.7 50.7 %reduce-scatter.5.cloned.1.call-done = f32[16,512]{1,0:T(8,128)} async-done(((f32[16,8192]{1,0:T(8,128)}), f32[16,512]{1,0:T(8,128)}) %reduce-scatter.5.cloned.1.call-update) | async-done | bytes 32784 | tf_op jit(solution)/shard_map/reduce_scatter | solution.py:220
  207.2 20.1 %all_gather.13 = bf16[16,8192]{1,0:T(8,128)(2,1)S(1)} all-gather(bf16[16,512]{1,0:T(8,128)(2,1)S(1)} %add_convert_fusion.6), channel_id=1, replica_groups=mesh['group'=2,'tensor'=16] {'tensor'}, dimensions={1}, use_global_device_ids=true | all-gather | bytes 278528 | tf_op jit(solution)/shard_map/all_gather | solution.py:183
  230.3 2.7 fusion.148
  234.6 57.8 %psum.29 = bf16[16,192]{1,0:T(8,128)(2,1)S(1)} all-reduce(f32[16,192]{1,0:T(8,128)S(1)} %broadcast_select_fusion.5), channel_id=1, replica_groups=mesh['group'=2,'tensor'=16] {'tensor'}, use_global_device_ids=true, to_apply=%region_16.25 | all-reduce | flops 3072 | bytes 18432 | tf_op jit(solution)/shard_map/psum | solution.py:188
  298.2 3.4 all-to-all-start.4
  301.7 2.0 fusion.136
  303.7 1.7 gather_fusion.12
  305.4 4.6 fusion.14
  311.2 6.0 all-to-all-start.3
  317.7 5.9 all-to-all-done.3
  327.3 9.1 %all_to_all.185 = bf16[16,2,256]{2,1,0:T(2,128)(2,1)S(1)} all-to-all(bf16[16,2,256]{2,1,0:T(2,128)(2,1)S(1)} %reshape.1753), channel_id=1, replica_groups=mesh['group'=2,'tensor'=16] {'tensor'}, dimensions={0} | all-to-all | bytes 32768 | tf_op jit(solution)/shard_map/all_to_all | solution.py:218
  336.4 5.4 fusion.80
  343.0 51.9 %reduce-scatter.7.cloned.1.call-done = f32[16,512]{1,0:T(8,128)} async-done(((f32[16,8192]{1,0:T(8,128)}), f32[16,512]{1,0:T(8,128)}) %reduce-scatter.7.cloned.1.call-update) | async-done | bytes 32784 | tf_op jit(solution)/shard_map/reduce_scatter | solution.py:220
  395.7 20.1 %all_gather.14 = bf16[16,8192]{1,0:T(8,128)(2,1)S(1)} all-gather(bf16[16,512]{1,0:T(8,128)(2,1)S(1)} %add_convert_fusion.4), channel_id=1, replica_groups=mesh['group'=2,'tensor'=16] {'tensor'}, dimensions={1}, use_global_device_ids=true | all-gather | bytes 278528 | tf_op jit(solution)/shard_map/all_gather | solution.py:183
  418.7 2.7 fusion.149
  423.1 57.8 %psum.30 = bf16[16,192]{1,0:T(8,128)(2,1)S(1)} all-reduce(f32[16,192]{1,0:T(8,128)S(1)} %broadcast_select_fusion.4), channel_id=1, replica_groups=mesh['group'=2,'tensor'=16] {'tensor'}, use_global_device_ids=true, to_apply=%region_23.32 | all-reduce | flops 3072 | bytes 18432 | tf_op jit(solution)/shard_map/psum | solution.py:188
  486.7 3.5 all-to-all-start.7
  490.2 2.0 fusion.135
  492.3 1.7 gather_fusion.18
  494.0 4.6 fusion.13
  499.8 6.0 all-to-all-start.6
  506.1 6.1 all-to-all-done.6
  517.7 9.1 %all_to_all.186 = bf16[16,2,256]{2,1,0:T(2,128)(2,1)S(1)} all-to-all(bf16[16,2,256]{2,1,0:T(2,128)(2,1)S(1)} %reshape.1757), channel_id=1, replica_groups=mesh['group'=2,'tensor'=16] {'tensor'}, dimensions={0} | all-to-all | bytes 32768 | tf_op jit(solution)/shard_map/all_to_all | solution.py:218
  526.8 5.4 fusion.77
  533.5 52.0 %reduce-scatter.9.cloned.1.call-done = f32[16,512]{1,0:T(8,128)} async-done(((f32[16,8192]{1,0:T(8,128)}), f32[16,512]{1,0:T(8,128)}) %reduce-scatter.9.cloned.1.call-update) | async-done | bytes 32784 | tf_op jit(solution)/shard_map/reduce_scatter | solution.py:220
  586.2 20.1 %all_gather.15 = bf16[16,8192]{1,0:T(8,128)(2,1)S(1)} all-gather(bf16[16,512]{1,0:T(8,128)(2,1)S(1)} %add_convert_fusion.2), channel_id=1, replica_groups=mesh['group'=2,'tensor'=16] {'tensor'}, dimensions={1}, use_global_device_ids=true | all-gather | bytes 278528 | tf_op jit(solution)/shard_map/all_gather | solution.py:183
  609.3 2.7 fusion.150
  613.7 57.8 %psum.31 = bf16[16,192]{1,0:T(8,128)(2,1)S(1)} all-reduce(f32[16,192]{1,0:T(8,128)S(1)} %broadcast_select_fusion.3), channel_id=1, replica_groups=mesh['group'=2,'tensor'=16] {'tensor'}, use_global_device_ids=true, to_apply=%region_30.39 | all-reduce | flops 3072 | bytes 18432 | tf_op jit(solution)/shard_map/psum | solution.py:188
  676.7 3.6 all-to-all-start.10
  680.4 2.0 fusion.134
  682.4 1.7 gather_fusion.24
  684.1 4.6 fusion.12
  689.9 5.8 all-to-all-start.9
  696.0 6.1 all-to-all-done.9
  706.4 9.1 %all_to_all.187 = bf16[16,2,256]{2,1,0:T(2,128)(2,1)S(1)} all-to-all(bf16[16,2,256]{2,1,0:T(2,128)(2,1)S(1)} %reshape.1761), channel_id=1, replica_groups=mesh['group'=2,'tensor'=16] {'tensor'}, dimensions={0} | all-to-all | bytes 32768 | tf_op jit(solution)/shard_map/all_to_all | solution.py:218
  715.5 5.4 fusion.74
  721.5 52.5 %reduce-scatter.11.cloned.1.call-done = f32[16,512]{1,0:T(8,128)} async-done(((f32[16,8192]{1,0:T(8,128)}), f32[16,512]{1,0:T(8,128)}) %reduce-scatter.11.cloned.1.call-update) | async-done | bytes 32784 | tf_op jit(solution)/shard_map/reduce_scatter | solution.py:220
  (291 shorter events, 78.3 us)
Async XLA Ops:
  7.2 97.5 %copy-start = (bf16[8192,128]{1,0:T(8,128)(2,1)S(1)}, bf16[8192,128]{1,0:T(8,128)(2,1)}, u32[]{:S(2)}) copy-start(bf16[8192,128]{1,0:T(8,128)(2,1)} %param.47) | copy-start | bytes 6291460
  10.0 219.3 %copy-start.13 = (pred[144]{0:T(512)(128)(4,1)}, pred[144]{0:T(512)(128)(4,1)S(1)}, u32[]{:S(2)}) copy-start(pred[144]{0:T(512)(128)(4,1)S(1)} %compare_and_fusion.1) | copy-start | bytes 436
  10.1 471.7 %copy-start.9 = (s32[1024]{0:T(1024)}, s32[1024]{0:T(1024)S(1)}, u32[]{:S(2)}) copy-start(s32[1024]{0:T(1024)S(1)} %pad_clamp_fusion.2) | copy-start | bytes 12292
  35.0 194.3 %copy-start.16 = (bf16[144]{0:T(256)(128)(2,1)}, bf16[144]{0:T(256)(128)(2,1)S(1)}, u32[]{:S(2)}) copy-start(bf16[144]{0:T(256)(128)(2,1)S(1)} %convert_element_type.316) | copy-start | bytes 868
  35.1 76.4 %copy-start.12 = (pred[9]{0:T(512)(128)(4,1)}, pred[9]{0:T(512)(128)(4,1)S(1)}, u32[]{:S(2)}) copy-start(pred[9]{0:T(512)(128)(4,1)S(1)} %get-tuple-element.112) | copy-start | bytes 31
  35.2 197.9 %copy-start.29 = (s32[1024]{0:T(1024)}, s32[1024]{0:T(1024)S(1)}, u32[]{:S(2)}) copy-start(s32[1024]{0:T(1024)S(1)} %pad_clamp_fusion) | copy-start | bytes 12292
  41.4 61.8 %copy-start.4 = (bf16[8,64,128]{2,1,0:T(8,128)(2,1)S(1)}, bf16[8,64,128]{2,1,0:T(8,128)(2,1)}, u32[]{:S(2)}) copy-start(bf16[8,64,128]{2,1,0:T(8,128)(2,1)} %param.51) | copy-start | bytes 393220
  103.7 8.1 %copy-start.3 = (bf16[9,64,128]{2,1,0:T(8,128)(2,1)}, bf16[9,64,128]{2,1,0:T(8,128)(2,1)S(1)}, u32[]{:S(2)}) copy-start(bf16[9,64,128]{2,1,0:T(8,128)(2,1)S(1)} %gather_fusion.7) | copy-start | bytes 442372
  105.7 17.0 %all-to-all-start.1 = ((bf16[16,1,128]{2,1,0:T(2,128)(2,1)}), bf16[16,1,128]{2,1,0:T(2,128)(2,1)S(1)}, u32[]{:S(2)}, u32[]{:S(2)}) async-start(bf16[16,1,128]{2,1,0:T(2,128)(2,1)} %copy.112), calls=%async_computation.1 | async-start | bytes 16384 | tf_op jit(solution)/shard_map/all_to_all | solution.py:94
  117.0 18.3 %copy-start.30 = (pred[512]{0:T(512)(128)(4,1)}, pred[512]{0:T(512)(128)(4,1)S(1)}, u32[]{:S(2)}) copy-start(pred[512]{0:T(512)(128)(4,1)S(1)} %iota_compare_fusion.4) | copy-start | bytes 1540
  122.7 12.5 %all-to-all-start = ((bf16[16,2,256]{2,1,0:T(2,128)(2,1)}), bf16[16,2,256]{2,1,0:T(2,128)(2,1)S(1)}, u32[]{:S(2)}, u32[]{:S(2)}) async-start(bf16[16,2,256]{2,1,0:T(2,128)(2,1)} %reshape.1747), calls=%async_computation | async-start | bytes 32768 | tf_op jit(solution)/shard_map/all_to_all | solution.py:93
  128.7 77.8 %reduce-scatter.5.cloned.1.call-start = ((), (), s32[]{:S(2)}) async-start(), calls=%async_computation.16 | async-start | bytes 557056 | tf_op jit(solution)/shard_map/reduce_scatter | solution.py:220
  147.8 58.7 %copy-start.11 = (bf16[16,512]{1,0:T(8,128)(2,1)S(1)}, bf16[16,512]{1,0:T(8,128)(2,1)}, u32[]{:S(2)}) copy-start(bf16[16,512]{1,0:T(8,128)(2,1)} %param.44) | copy-start | bytes 49156
  207.2 20.3 %copy-start.7 = (bf16[16,512]{1,0:T(8,128)(2,1)}, bf16[16,512]{1,0:T(8,128)(2,1)S(1)}, u32[]{:S(2)}) copy-start(bf16[16,512]{1,0:T(8,128)(2,1)S(1)} %add_convert_fusion.6) | copy-start | bytes 49156
  298.2 13.0 %all-to-all-start.4 = ((bf16[16,1,128]{2,1,0:T(2,128)(2,1)}), bf16[16,1,128]{2,1,0:T(2,128)(2,1)S(1)}, u32[]{:S(2)}, u32[]{:S(2)}) async-start(bf16[16,1,128]{2,1,0:T(2,128)(2,1)} %copy.119), calls=%async_computation.5 | async-start | bytes 16384 | tf_op jit(solution)/shard_map/all_to_all | solution.py:94
  305.4 11.9 %copy-start.35 = (f32[64]{0:T(128)S(1)}, f32[64]{0:T(128)}, u32[]{:S(2)}) copy-start(f32[64]{0:T(128)} %get-tuple-element.172) | copy-start | bytes 772
  305.4 11.9 %copy-start.36 = (f32[64]{0:T(128)S(1)}, f32[64]{0:T(128)}, u32[]{:S(2)}) copy-start(f32[64]{0:T(128)} %get-tuple-element.173) | copy-start | bytes 772
  305.4 12.1 %copy-start.24 = (bf16[1,4,8,128]{3,1,2,0:T(4,128)(2,1)S(1)}, bf16[1,4,8,128]{3,1,2,0:T(4,128)(2,1)}, u32[]{:S(2)}) copy-start(bf16[1,4,8,128]{3,1,2,0:T(4,128)(2,1)} %scatter.29) | copy-start | bytes 24580
  305.4 12.1 %copy-start.19 = (bf16[1,4,8,128]{3,1,2,0:T(4,128)(2,1)S(1)}, bf16[1,4,8,128]{3,1,2,0:T(4,128)(2,1)}, u32[]{:S(2)}) copy-start(bf16[1,4,8,128]{3,1,2,0:T(4,128)(2,1)} %fusion.90) | copy-start | bytes 24580
  305.4 18.4 %copy-start.31 = (pred[512]{0:T(512)(128)(4,1)S(1)}, pred[512]{0:T(512)(128)(4,1)}, u32[]{:S(2)}) copy-start(pred[512]{0:T(512)(128)(4,1)} %copy-done.30) | copy-start | bytes 1540
  305.4 18.9 %copy-start.39 = (pred[4]{0:T(512)(128)(4,1)S(1)}, pred[4]{0:T(512)(128)(4,1)}, u32[]{:S(2)}) copy-start(pred[4]{0:T(512)(128)(4,1)} %iota_compare_fusion.7) | copy-start | bytes 16
  311.2 12.5 %all-to-all-start.3 = ((bf16[16,2,256]{2,1,0:T(2,128)(2,1)}), bf16[16,2,256]{2,1,0:T(2,128)(2,1)S(1)}, u32[]{:S(2)}, u32[]{:S(2)}) async-start(bf16[16,2,256]{2,1,0:T(2,128)(2,1)} %reshape.1751), calls=%async_computation.4 | async-start | bytes 32768 | tf_op jit(solution)/shard_map/all_to_all | solution.py:93
  317.2 77.7 %reduce-scatter.7.cloned.1.call-start = ((), (), s32[]{:S(2)}) async-start(), calls=%async_computation.17 | async-start | bytes 557056 | tf_op jit(solution)/shard_map/reduce_scatter | solution.py:220
  317.5 24.2 %copy-start.25 = (bf16[1,4,8,128]{3,1,2,0:T(4,128)(2,1)}, bf16[1,4,8,128]{3,1,2,0:T(4,128)(2,1)S(1)}, u32[]{:S(2)}) copy-start(bf16[1,4,8,128]{3,1,2,0:T(4,128)(2,1)S(1)} %scatter.31) | copy-start | bytes 24580
  317.7 24.0 %copy-start.20 = (bf16[1,4,8,128]{3,1,2,0:T(4,128)(2,1)}, bf16[1,4,8,128]{3,1,2,0:T(4,128)(2,1)S(1)}, u32[]{:S(2)}) copy-start(bf16[1,4,8,128]{3,1,2,0:T(4,128)(2,1)S(1)} %scatter.30) | copy-start | bytes 24580
  336.3 58.5 %copy-start.8 = (bf16[16,512]{1,0:T(8,128)(2,1)S(1)}, bf16[16,512]{1,0:T(8,128)(2,1)}, u32[]{:S(2)}) copy-start(bf16[16,512]{1,0:T(8,128)(2,1)} %copy-done.7) | copy-start | bytes 49156
  341.8 75.9 %copy-start.14 = (pred[144]{0:T(512)(128)(4,1)S(1)}, pred[144]{0:T(512)(128)(4,1)}, u32[]{:S(2)}) copy-start(pred[144]{0:T(512)(128)(4,1)} %copy-done.13) | copy-start | bytes 436
  341.8 75.9 %copy-start.17 = (bf16[144]{0:T(256)(128)(2,1)S(1)}, bf16[144]{0:T(256)(128)(2,1)}, u32[]{:S(2)}) copy-start(bf16[144]{0:T(256)(128)(2,1)} %copy-done.16) | copy-start | bytes 868
  486.7 13.0 %all-to-all-start.7 = ((bf16[16,1,128]{2,1,0:T(2,128)(2,1)}), bf16[16,1,128]{2,1,0:T(2,128)(2,1)S(1)}, u32[]{:S(2)}, u32[]{:S(2)}) async-start(bf16[16,1,128]{2,1,0:T(2,128)(2,1)} %copy.126), calls=%async_computation.9 | async-start | bytes 16384 | tf_op jit(solution)/shard_map/all_to_all | solution.py:94
  494.0 11.9 %copy-start.37 = (f32[64]{0:T(128)S(1)}, f32[64]{0:T(128)}, u32[]{:S(2)}) copy-start(f32[64]{0:T(128)} %get-tuple-element.174) | copy-start | bytes 772
  494.0 11.9 %copy-start.38 = (f32[64]{0:T(128)S(1)}, f32[64]{0:T(128)}, u32[]{:S(2)}) copy-start(f32[64]{0:T(128)} %get-tuple-element.175) | copy-start | bytes 772
  494.0 12.0 %copy-start.26 = (bf16[1,4,8,128]{3,1,2,0:T(4,128)(2,1)S(1)}, bf16[1,4,8,128]{3,1,2,0:T(4,128)(2,1)}, u32[]{:S(2)}) copy-start(bf16[1,4,8,128]{3,1,2,0:T(4,128)(2,1)} %copy-done.25) | copy-start | bytes 24580
  494.0 12.1 %copy-start.21 = (bf16[1,4,8,128]{3,1,2,0:T(4,128)(2,1)S(1)}, bf16[1,4,8,128]{3,1,2,0:T(4,128)(2,1)}, u32[]{:S(2)}) copy-start(bf16[1,4,8,128]{3,1,2,0:T(4,128)(2,1)} %copy-done.20) | copy-start | bytes 24580
  499.8 12.5 %all-to-all-start.6 = ((bf16[16,2,256]{2,1,0:T(2,128)(2,1)}), bf16[16,2,256]{2,1,0:T(2,128)(2,1)S(1)}, u32[]{:S(2)}, u32[]{:S(2)}) async-start(bf16[16,2,256]{2,1,0:T(2,128)(2,1)} %reshape.1755), calls=%async_computation.8 | async-start | bytes 32768 | tf_op jit(solution)/shard_map/all_to_all | solution.py:93
  505.8 79.7 %reduce-scatter.9.cloned.1.call-start = ((), (), s32[]{:S(2)}) async-start(), calls=%async_computation.18 | async-start | bytes 557056 | tf_op jit(solution)/shard_map/reduce_scatter | solution.py:220
  506.1 26.2 %copy-start.27 = (bf16[1,4,8,128]{3,1,2,0:T(4,128)(2,1)}, bf16[1,4,8,128]{3,1,2,0:T(4,128)(2,1)S(1)}, u32[]{:S(2)}) copy-start(bf16[1,4,8,128]{3,1,2,0:T(4,128)(2,1)S(1)} %scatter.35) | copy-start | bytes 24580
  506.1 26.1 %copy-start.22 = (bf16[1,4,8,128]{3,1,2,0:T(4,128)(2,1)}, bf16[1,4,8,128]{3,1,2,0:T(4,128)(2,1)S(1)}, u32[]{:S(2)}) copy-start(bf16[1,4,8,128]{3,1,2,0:T(4,128)(2,1)S(1)} %scatter.34) | copy-start | bytes 24580
  526.8 79.9 %copy-start.10 = (s32[1024]{0:T(1024)S(1)}, s32[1024]{0:T(1024)}, u32[]{:S(2)}) copy-start(s32[1024]{0:T(1024)} %copy-done.9) | copy-start | bytes 12292
  532.2 76.1 %copy-start.15 = (pred[144]{0:T(512)(128)(4,1)S(1)}, pred[144]{0:T(512)(128)(4,1)}, u32[]{:S(2)}) copy-start(pred[144]{0:T(512)(128)(4,1)} %copy-done.13) | copy-start | bytes 436
  532.2 76.1 %copy-start.18 = (bf16[144]{0:T(256)(128)(2,1)S(1)}, bf16[144]{0:T(256)(128)(2,1)}, u32[]{:S(2)}) copy-start(bf16[144]{0:T(256)(128)(2,1)} %copy-done.16) | copy-start | bytes 868
  676.7 13.2 %all-to-all-start.10 = ((bf16[16,1,128]{2,1,0:T(2,128)(2,1)}), bf16[16,1,128]{2,1,0:T(2,128)(2,1)S(1)}, u32[]{:S(2)}, u32[]{:S(2)}) async-start(bf16[16,1,128]{2,1,0:T(2,128)(2,1)} %copy.133), calls=%async_computation.13 | async-start | bytes 16384 | tf_op jit(solution)/shard_map/all_to_all | solution.py:94
  684.1 11.7 %copy-start.33 = (f32[64]{0:T(128)S(1)}, f32[64]{0:T(128)}, u32[]{:S(2)}) copy-start(f32[64]{0:T(128)} %get-tuple-element.176) | copy-start | bytes 772
  684.1 11.7 %copy-start.34 = (f32[64]{0:T(128)S(1)}, f32[64]{0:T(128)}, u32[]{:S(2)}) copy-start(f32[64]{0:T(128)} %get-tuple-element.177) | copy-start | bytes 772
  684.1 11.8 %copy-start.28 = (bf16[1,4,8,128]{3,1,2,0:T(4,128)(2,1)S(1)}, bf16[1,4,8,128]{3,1,2,0:T(4,128)(2,1)}, u32[]{:S(2)}) copy-start(bf16[1,4,8,128]{3,1,2,0:T(4,128)(2,1)} %copy-done.27) | copy-start | bytes 24580
  684.1 11.9 %copy-start.23 = (bf16[1,4,8,128]{3,1,2,0:T(4,128)(2,1)S(1)}, bf16[1,4,8,128]{3,1,2,0:T(4,128)(2,1)}, u32[]{:S(2)}) copy-start(bf16[1,4,8,128]{3,1,2,0:T(4,128)(2,1)} %copy-done.22) | copy-start | bytes 24580
  684.1 18.2 %copy-start.32 = (pred[512]{0:T(512)(128)(4,1)S(1)}, pred[512]{0:T(512)(128)(4,1)}, u32[]{:S(2)}) copy-start(pred[512]{0:T(512)(128)(4,1)} %copy-done.30) | copy-start | bytes 1540
  689.9 12.3 %all-to-all-start.9 = ((bf16[16,2,256]{2,1,0:T(2,128)(2,1)}), bf16[16,2,256]{2,1,0:T(2,128)(2,1)S(1)}, u32[]{:S(2)}, u32[]{:S(2)}) async-start(bf16[16,2,256]{2,1,0:T(2,128)(2,1)} %reshape.1759), calls=%async_computation.12 | async-start | bytes 32768 | tf_op jit(solution)/shard_map/all_to_all | solution.py:93
  695.7 78.3 %reduce-scatter.11.cloned.1.call-start = ((), (), s32[]{:S(2)}) async-start(), calls=%async_computation.19 | async-start | bytes 557056 | tf_op jit(solution)/shard_map/reduce_scatter | solution.py:220
  (4 other events, 15.6 us)
Sparse Core Ops, SparseCore 0:
  153.4 53.0 reduce-scatter.4
  341.9 52.9 reduce-scatter.6
  532.4 53.0 reduce-scatter.8
  721.0 52.9 reduce-scatter.10
where the time goes:
time: 784 us; the launch traced here: 782 us
  blocking collectives  352 us (45%)
  waiting for transfers between devices  232 us (30%)
  matrix products  72 us (9%)
  local copies, waits for them, and re-layouts  42.7 us (5%)
  starting transfers between devices  37.8 us (5%)
  other arithmetic  30.1 us (4%)
  between operations  15.5 us (2%)
    psum x4, blocking collectives, body(): lax.psum(split_into_blocks(normalized_portion, adapter_down_weight, page_...  231 us
    reduce_scatter x4, waiting for transfers between devices, body(): lax.psum_scatter(out_term, 'tensor', scatter_dimension=1, tiled=True)  207 us
    all_gather x4, blocking collectives, body(): gathered = lax.all_gather(hidden_state, 'tensor', axis=1, tiled=True)  84.4 us
    all_to_all x4, blocking collectives, body(): lax.all_to_all(attended_rows, 'tensor', split_axis=1, concat_axis=0, tile...  36.3 us
    all_to_all x4, waiting for transfers between devices, attend(): lax.all_to_all(query_projected, 'tensor', split_axis=0, concat_axis=1, ti...  24.5 us
    all_to_all x4, starting transfers between devices, attend(): lax.all_to_all(query_projected, 'tensor', split_axis=0, concat_axis=1, ti...  23.7 us
    dot_general x4, matrix products, body(): jnp.dot(attended, output_weight, preferred_element_type=jnp.float32)  21.6 us
    dot_general x12, matrix products, split_into_blocks(): jnp.einsum('bsk,bkm->bsm', gathered, chosen, preferred_element_type=jnp.f...  18.7 us
  transfers between devices with their start and end apart: 12, of which 8 were waited for; matrix products, arithmetic and copies ran while one was open for 6% of the time, Pallas kernels for 0%

commit v1 on v0

--- a/solution.py
+++ b/solution.py
@@ -1,6 +1,10 @@
+import functools
+
 import jax
 import jax.numpy as jnp
 from jax import lax
+from jax.experimental import pallas as pl
+from jax.experimental.pallas import tpu as pltpu
 from jax.sharding import PartitionSpec as P
 
 QUERY_HEADS = 64
@@ -16,6 +20,12 @@
 eps = 1e-05
 rope_base = 500000.0
 adapter_scale = 0.5
+MESH = pl.DeviceIdType.MESH
+F32 = jnp.float32
+BF16 = jnp.bfloat16
+WEIGHT_PIECES = 4
+PADDED_HEADS = 8
+PARTIAL_TYPE = jnp.float32
 
 
 def apply_rotary(values_in, token_positions):
@@ -229,6 +239,505 @@
     return (hidden_state, new_keyval)
 
 
+def dot(a, b):
+    return jnp.dot(a, b, preferred_element_type=F32)
+
+
+def decode_kernel(
+    n,
+    residual,
+    gain,
+    row_adapter,
+    cosine,
+    sine,
+    bias,
+    wq_hbm,
+    wkv_hbm,
+    wo_hbm,
+    down_hbm,
+    upq_hbm,
+    upkv_hbm,
+    kc_hbm,
+    vc_hbm,
+    hidden_out,
+    keyval_out,
+    wq,
+    wkv,
+    wo,
+    down,
+    upq,
+    upkv,
+    kc,
+    vc,
+    hidden,
+    gathered,
+    normed,
+    dn_send,
+    dn_recv,
+    qkv_send,
+    qkv_recv,
+    att_send,
+    att_recv,
+    pair_send,
+    pair_recv,
+    chip_send,
+    chip_recv,
+    kept,
+    wq_sem,
+    wkv_sem,
+    load_sem,
+    ag_send_sem,
+    ag_fwd_sem,
+    ag_recv_sem,
+    dn_send_sem,
+    dn_recv_sem,
+    qkv_send_sem,
+    qkv_recv_sem,
+    att_send_sem,
+    att_recv_sem,
+    pair_send_sem,
+    pair_recv_sem,
+    chip_send_sem,
+    chip_recv_sem,
+):
+    rows, width = residual.shape
+    model = n * width
+    head = HEAD_SIZE
+    query_blocks = width // head
+    chips = n // 2
+    me = lax.axis_index("tensor")
+    core = lax.rem(me, 2)
+    chip = lax.div(me, 2)
+    partner = me + 1 - 2 * core
+    piece = model // WEIGHT_PIECES
+
+    def wq_load(i):
+        part = pl.ds(i * piece, piece)
+        return pltpu.make_async_copy(wq_hbm.at[part], wq.at[part], wq_sem.at[i])
+
+    def wkv_load(i):
+        part = pl.ds(i * piece, piece)
+        return pltpu.make_async_copy(wkv_hbm.at[part], wkv.at[part], wkv_sem.at[i])
+
+    def load(source, target, i):
+        return pltpu.make_async_copy(source, target, load_sem.at[i])
+
+    down_load = load(down_hbm, down, 0)
+    upq_load = load(upq_hbm, upq, 1)
+    upkv_load = load(upkv_hbm, upkv, 2)
+    kc_load = load(kc_hbm, kc, 3)
+    vc_load = load(vc_hbm, vc, 4)
+    wo_load = load(wo_hbm, wo, 5)
+
+    down_load.start()
+    for i in range(WEIGHT_PIECES):
+        wq_load(i).start()
+        wkv_load(i).start()
+    for copy in (upq_load, upkv_load, kc_load, vc_load, wo_load):
+        copy.start()
+
+    def loop(low, high, action):
+        def step(k, carry):
+            action(k)
+            return carry
+
+        lax.fori_loop(low, high, step, 0)
+
+    barrier = pltpu.get_barrier_semaphore()
+
+    def greet(k):
+        pl.semaphore_signal(
+            barrier, inc=1, device_id={"tensor": lax.rem(me + k, n)}, device_id_type=MESH
+        )
+
+    loop(1, n, greet)
+
+    hidden[...] = residual[...]
+    qkv_send[...] = jnp.zeros_like(qkv_send)
+    pl.semaphore_wait(barrier, n - 1)
+
+    def remote(source, target, send, recv, device):
+        return pltpu.make_async_remote_copy(
+            src_ref=source,
+            dst_ref=target,
+            send_sem=send,
+            recv_sem=recv,
+            device_id={"tensor": device},
+            device_id_type=MESH,
+        )
+
+    def chip_after(k):
+        return lax.rem(chip + k, chips)
+
+    def chip_before(k):
+        return lax.rem(chip + chips - k, chips)
+
+    def ag_direct(k):
+        return remote(
+            hidden,
+            gathered.at[me],
+            ag_send_sem.at[k],
+            ag_recv_sem.at[me],
+            2 * chip_after(k) + core,
+        )
+
+    def ag_pair():
+        return remote(hidden, gathered.at[me], ag_send_sem.at[0], ag_recv_sem.at[me], partner)
+
+    def ag_arrival(source):
+        return remote(
+            hidden, gathered.at[source], ag_send_sem.at[0], ag_recv_sem.at[source], partner
+        )
+
+    def ag_forward(k):
+        source = 2 * chip_before(k) + core
+        return remote(
+            gathered.at[source],
+            gathered.at[source],
+            ag_fwd_sem.at[k],
+            ag_recv_sem.at[source],
+            partner,
+        )
+
+    def exchange(send, recv, send_sem, recv_sem, unit):
+        def block(ref, i):
+            return ref.at[pl.ds(pl.multiple_of(i * unit, unit), unit)]
+
+        def outgoing(k):
+            target = lax.rem(me + k, n)
+            return remote(
+                block(send, target), block(recv, me), send_sem.at[k], recv_sem.at[me], target
+            )
+
+        def incoming(k):
+            source = lax.rem(me + n - k, n)
+            return remote(
+                block(send, source), block(recv, source), send_sem.at[k], recv_sem.at[source], source
+            )
+
+        def start():
+            loop(1, n, lambda k: outgoing(k).start())
+            own = pl.ds(pl.multiple_of(me * unit, unit), unit)
+            recv[own, :] = send[own, :]
+
+        def finish():
+            loop(1, n, lambda k: incoming(k).wait_recv())
+            loop(1, n, lambda k: outgoing(k).wait_send())
+
+        return start, finish
+
+    qkv_start, qkv_finish = exchange(qkv_send, qkv_recv, qkv_send_sem, qkv_recv_sem, PADDED_HEADS)
+    att_start, att_finish = exchange(att_send, att_recv, att_send_sem, att_recv_sem, PADDED_HEADS)
+
+    def dn_out(k):
+        target = lax.rem(me + k, n)
+        half = lax.div(target, n // 2)
+        return remote(
+            dn_send.at[half], dn_recv.at[me], dn_send_sem.at[k], dn_recv_sem.at[me], target
+        )
+
+    def dn_in(k):
+        source = lax.rem(me + n - k, n)
+        return remote(
+            dn_send.at[0], dn_recv.at[source], dn_send_sem.at[k], dn_recv_sem.at[source], source
+        )
+
+    def pair_copy(j):
+        return remote(
+            pair_send.at[j], pair_recv.at[j], pair_send_sem.at[j], pair_recv_sem.at[j], partner
+        )
+
+    def chip_copy(j):
+        return remote(
+            chip_send.at[j],
+            chip_recv.at[j],
+            chip_send_sem.at[j],
+            chip_recv_sem.at[j],
+            2 * chip_after(j + 1) + core,
+        )
+
+    adapter = row_adapter[...]
+
+    def spread(values):
+        twice = jnp.concatenate([values, values], axis=1)
+        lane = lax.broadcasted_iota(jnp.int32, twice.shape, 1)
+        second = (lane >= ADAPTER_RANK).astype(jnp.int32)
+        parts = [
+            jnp.where(adapter == second + 2 * j, twice, jnp.zeros_like(twice))
+            for j in range(ADAPTER_COUNT // 2)
+        ]
+        return jnp.concatenate(parts, axis=1).astype(BF16)
+
+    def decode_step(t):
+        first = t == 0
+        loop(1, chips, lambda k: ag_direct(k).start())
+        ag_pair().start()
+        gathered[me] = hidden[...]
+
+        def pass_on(k):
+            ag_arrival(2 * chip_before(k) + core).wait_recv()
+            ag_forward(k).start()
+
+        loop(1, chips, pass_on)
+        loop(0, chips, lambda k: ag_arrival(2 * chip_before(k) + 1 - core).wait_recv())
+
+        total = jnp.zeros((rows, width), F32)
+        for k in range(n):
+            block = gathered[k].astype(F32)
+            total = total + block * block
+        scale = lax.rsqrt(jnp.sum(total, axis=1, keepdims=True) * (1.0 / model) + eps)
+
+        mine = pl.ds(pl.multiple_of(me * width, width), width)
+        own = (hidden[...].astype(F32) * scale * gain[:, mine]).astype(BF16)
+
+        @pl.when(first)
+        def _():
+            down_load.wait()
+
+        partial = jnp.zeros((rows, down.shape[2]), F32)
+        for a in range(ADAPTER_COUNT):
+            partial = partial + jnp.where(adapter == a, dot(own, down[a]), 0.0)
+        for_query = partial[:, :ADAPTER_RANK]
+        dn_send[0] = partial[:, : 2 * ADAPTER_RANK]
+        dn_send[1] = jnp.concatenate([for_query, partial[:, 2 * ADAPTER_RANK :]], axis=1)
+        loop(1, n, lambda k: dn_out(k).start())
+        dn_recv[me] = dn_send[lax.div(me, n // 2)]
+
+        for k in range(n):
+            block = gathered[k].astype(F32)
+            here = slice(k * width, (k + 1) * width)
+            normed[:, here] = (block * scale * gain[:, here]).astype(BF16)
+
+        query = jnp.zeros((rows, width), F32)
+        keyval = jnp.zeros((rows, wkv.shape[1]), F32)
+        for i in range(WEIGHT_PIECES):
+
+            @pl.when(first)
+            def _():
+                wq_load(i).wait()
+                wkv_load(i).wait()
+
+            here = slice(i * piece, (i + 1) * piece)
+            part = normed[:, here]
+            query = query + dot(part, wq[here, :])
+            keyval = keyval + dot(part, wkv[here, :])
+
+        @pl.when(first)
+        def _():
+            upq_load.wait()
+            upkv_load.wait()
+
+        loop(1, n, lambda k: dn_in(k).wait_recv())
+        shrunk = dn_recv[0]
+        for k in range(1, n):
+            shrunk = shrunk + dn_recv[k]
+        shrunk = shrunk.astype(BF16).astype(F32)
+        query = query + adapter_scale * dot(spread(shrunk[:, :ADAPTER_RANK]), upq[...])
+        keyval = keyval + adapter_scale * dot(spread(shrunk[:, ADAPTER_RANK:]), upkv[...])
+        query = query.astype(BF16).astype(F32)
+        for h in range(query_blocks):
+            qkv_send[pl.ds(h, rows, stride=PADDED_HEADS), :] = query[:, h * head : (h + 1) * head]
+        qkv_send[pl.ds(query_blocks, rows, stride=PADDED_HEADS), :] = keyval.astype(BF16).astype(F32)
+        qkv_start()
+        loop(1, n, lambda k: dn_out(k).wait_send())
+        loop(1, chips, lambda k: ag_direct(k).wait_send())
+        loop(1, chips, lambda k: ag_forward(k).wait_send())
+        ag_pair().wait_send()
+
+        @pl.when(first)
+        def _():
+            kc_load.wait()
+            vc_load.wait()
+
+        qkv_finish()
+
+        raw = qkv_recv[...]
+        cos_row = cosine[pl.ds(t, 1), :]
+        sin_row = sine[pl.ds(t, 1), :]
+        rotated = raw * cos_row + pltpu.roll(raw, head // 2, 1) * sin_row
+        bias_row = bias[pl.ds(t, 1), :]
+        capacity = kc.shape[0]
+        tail = slice(capacity - 16, capacity)
+        sub = lax.broadcasted_iota(jnp.int32, (16, head), 0)
+        fresh = sub == 16 - DECODE_STEPS + t
+        for g in range(KEY_VALUE_HEADS):
+            here = slice(g * head, (g + 1) * head)
+            at_key = PADDED_HEADS * g + query_blocks
+            at_value = PADDED_HEADS * (n // 2 + g) + query_blocks
+            new_key = rotated[at_key : at_key + 1, :]
+            new_value = raw[at_value : at_value + 1, :]
+            kc[tail, here] = jnp.where(fresh, new_key, kc[tail, here].astype(F32)).astype(BF16)
+            vc[tail, here] = jnp.where(fresh, new_value, vc[tail, here].astype(F32)).astype(BF16)
+        for g in range(KEY_VALUE_HEADS):
+            here = slice(g * head, (g + 1) * head)
+            heads = slice(2 * PADDED_HEADS * g, 2 * PADDED_HEADS * (g + 1))
+            scores = lax.dot_general(
+                rotated[heads, :].astype(BF16),
+                kc[:, here],
+                (((1,), (1,)), ((), ())),
+                preferred_element_type=F32,
+            )
+            scores = scores * head ** (-0.5) + bias_row
+            top = jnp.max(scores, axis=1, keepdims=True)
+            powers = jnp.exp(scores - top)
+            weights = powers / jnp.sum(powers, axis=1, keepdims=True)
+            att_send[heads, :] = dot(weights.astype(BF16), vc[:, here]).astype(BF16).astype(F32)
+        att_start()
+
+        @pl.when(first)
+        def _():
+            wo_load.wait()
+
+        att_finish()
+        attended = jnp.concatenate(
+            [att_recv[pl.ds(h, rows, stride=PADDED_HEADS), :] for h in range(query_blocks)], axis=1
+        ).astype(BF16)
+
+        def product(device):
+            return dot(attended, wo[:, pl.ds(pl.multiple_of(device * width, width), width)])
+
+        for j in range(chips):
+            pair_send[j] = product(2 * chip_after(j + 1) + 1 - core)
+            pair_copy(j).start()
+        for j in range(chips):
+            part = product(2 * chip_after(j + 1) + core)
+            pair_copy(j).wait_recv()
+            part = part + pair_recv[j]
+            if j < chips - 1:
+                chip_send[j] = part.astype(chip_send.dtype)
+                chip_copy(j).start()
+            else:
+                kept[...] = part
+        summed = kept[...]
+        for j in range(chips - 1):
+            chip_copy(j).wait_recv()
+            summed = summed + chip_recv[j].astype(F32)
+        hidden[...] = (hidden[...].astype(F32) + summed).astype(BF16)
+        loop(0, chips, lambda j: pair_copy(j).wait_send())
+        loop(0, chips - 1, lambda j: chip_copy(j).wait_send())
+
+    loop(0, DECODE_STEPS, decode_step)
+    hidden_out[...] = hidden[...]
+    end = kc.shape[0]
+    keys = kc[end - 16 : end, :].astype(F32)
+    values = vc[end - 16 : end, :].astype(F32)
+    both = jnp.concatenate([keys, values], axis=1)
+    keyval_out[...] = both[16 - DECODE_STEPS :, :].astype(BF16)
+
+
+def fused_body(
+    residual_input,
+    attention_norm_gain,
+    query_weight,
+    key_value_weight,
+    output_weight,
+    adapter_down_weight,
+    adapter_up_query,
+    adapter_up_key_value,
+    stored_key_cache,
+    stored_value_cache,
+    row_adapter_index,
+    cache_live_length,
+):
+    n = lax.axis_size("tensor")
+    rows, width = residual_input.shape
+    model, kv_cols = key_value_weight.shape
+    chips = n // 2
+    steps = jnp.arange(DECODE_STEPS, dtype=jnp.int32)
+    positions = cache_live_length[0] + steps
+    halfway = HEAD_SIZE // 2
+    frequency = rope_base ** (-jnp.arange(halfway, dtype=F32) / halfway)
+    angles = positions.astype(F32)[:, None] * frequency[None, :]
+    cosine = jnp.cos(angles)
+    sine = jnp.sin(angles)
+    cosine = jnp.concatenate([cosine, cosine], axis=1)
+    sine = jnp.concatenate([-sine, sine], axis=1)
+    capacity = stored_key_cache.shape[1]
+    slots = jnp.arange(capacity, dtype=jnp.int32)
+    newest = capacity - DECODE_STEPS
+    live = (slots[None, :] < jnp.minimum(cache_live_length, newest)[:, None]) | (
+        (slots[None, :] >= newest) & (slots[None, :] <= newest + steps[:, None])
+    )
+    bias = jnp.where(live, 0.0, -jnp.inf).astype(F32)
+    rank_rows = ADAPTER_COUNT * ADAPTER_RANK
+    vmem = pl.BlockSpec(memory_space=pltpu.VMEM)
+    hbm = pl.BlockSpec(memory_space=pl.ANY)
+    dma = pltpu.SemaphoreType.DMA
+    key_width = stored_key_cache.shape[2]
+    hidden_out, keyval_out = pl.pallas_call(
+        functools.partial(decode_kernel, n),
+        out_shape=(
+            jax.ShapeDtypeStruct((rows, width), BF16),
+            jax.ShapeDtypeStruct((DECODE_STEPS, 2 * key_width), BF16),
+        ),
+        in_specs=[vmem] * 6 + [hbm] * 8,
+        out_specs=(vmem, vmem),
+        scratch_shapes=[
+            pltpu.VMEM(query_weight.shape, BF16),
+            pltpu.VMEM(key_value_weight.shape, BF16),
+            pltpu.VMEM(output_weight.shape, BF16),
+            pltpu.VMEM(adapter_down_weight.shape, BF16),
+            pltpu.VMEM((rank_rows, width), BF16),
+            pltpu.VMEM((rank_rows, kv_cols), BF16),
+            pltpu.VMEM((capacity, key_width), BF16),
+            pltpu.VMEM((capacity, key_width), BF16),
+            pltpu.VMEM((rows, width), BF16),
+            pltpu.VMEM((n, rows, width), BF16),
+            pltpu.VMEM((rows, model), BF16),
+            pltpu.VMEM((2, rows, 2 * ADAPTER_RANK), F32),
+            pltpu.VMEM((n, rows, 2 * ADAPTER_RANK), F32),
+            pltpu.VMEM((n * PADDED_HEADS, HEAD_SIZE), F32),
+            pltpu.VMEM((n * PADDED_HEADS, HEAD_SIZE), F32),
+            pltpu.VMEM((n * PADDED_HEADS, HEAD_SIZE), F32),
+            pltpu.VMEM((n * PADDED_HEADS, HEAD_SIZE), F32),
+            pltpu.VMEM((chips, rows, width), F32),
+            pltpu.VMEM((chips, rows, width), F32),
+            pltpu.VMEM((chips - 1, rows, width), PARTIAL_TYPE),
+            pltpu.VMEM((chips - 1, rows, width), PARTIAL_TYPE),
+            pltpu.VMEM((rows, width), F32),
+            dma((WEIGHT_PIECES,)),
+            dma((WEIGHT_PIECES,)),
+            dma((6,)),
+            dma((chips,)),
+            dma((chips,)),
+            dma((n,)),
+            dma((n,)),
+            dma((n,)),
+            dma((n,)),
+            dma((n,)),
+            dma((n,)),
+            dma((n,)),
+            dma((chips,)),
+            dma((chips,)),
+            dma((chips - 1,)),
+            dma((chips - 1,)),
+        ],
+        compiler_params=pltpu.CompilerParams(
+            collective_id=0, has_side_effects=True, vmem_limit_bytes=56 * 1024 * 1024
+        ),
+    )(
+        residual_input,
+        attention_norm_gain.astype(F32).reshape(1, model),
+        row_adapter_index.reshape(rows, 1),
+        cosine,
+        sine,
+        bias,
+        query_weight,
+        key_value_weight,
+        output_weight,
+        adapter_down_weight,
+        adapter_up_query.reshape(rank_rows, width),
+        adapter_up_key_value.reshape(rank_rows, kv_cols),
+        stored_key_cache.reshape(capacity, key_width),
+        stored_value_cache.reshape(capacity, key_width),
+    )
+    return (hidden_out, keyval_out[None])
+
+
+def fits_fused(mesh):
+    return mesh.shape["tensor"] == 2 * KEY_VALUE_HEADS
+
+
 def solution(mesh):
     in_specs = (
         P("group", "tensor"),
@@ -245,4 +754,5 @@
         P(("group", "tensor")),
     )
     out_specs = (P("group", "tensor"), P(("group", "tensor"), None, None))
-    return jax.shard_map(body, mesh=mesh, in_specs=in_specs, out_specs=out_specs, check_vma=False)
+    run = fused_body if fits_fused(mesh) else body
+    return jax.shard_map(run, mesh=mesh, in_specs=in_specs, out_specs=out_specs, check_vma=False)

time: 784 us -> 148 us (0.19)
  blocking collectives: 352 us -> 0 us
  waiting for transfers between devices: 232 us -> 0 us
  Pallas kernels: 0 us -> 136 us
  matrix products: 72 us -> 0 us
  starting transfers between devices: 37.8 us -> 0 us
  local copies, waits for them, and re-layouts: 42.7 us -> 7.67 us
  other arithmetic: 30.1 us -> 2.8 us
  between operations: 15.5 us -> 1.31 us
    psum x4 -> x0, blocking collectives: 231 us -> none  [body(): lax.psum(split_into_blocks(normalized_portion, adapter_down_weight, page_...]
    reduce_scatter x4 -> x0, waiting for transfers between devices: 207 us -> none  [body(): lax.psum_scatter(out_term, 'tensor', scatter_dimension=1, tiled=True)]
    pallas_call x0 -> x1, Pallas kernels: none -> 136 us  [fused_body(): pl.pallas_call(functools.partial(decode_kernel, n), out_shape=(jax.ShapeD...]
    all_gather x4 -> x0, blocking collectives: 84.4 us -> none  [body(): gathered = lax.all_gather(hidden_state, 'tensor', axis=1, tiled=True)]
    dot_general x40 -> x0, matrix products: 72 us -> none  [the longest x4 21.6 us: body(): jnp.dot(attended, output_weight, preferred_element_type=jnp.float32)]
    all_to_all x8 -> x0, starting transfers between devices: 37.7 us -> none  [the longest x4 23.7 us: attend(): lax.all_to_all(query_projected, 'tensor', split_axis=0, concat_axis=1, ti...]
    all_to_all x4 -> x0, blocking collectives: 36.3 us -> none  [body(): lax.all_to_all(attended_rows, 'tensor', split_axis=1, concat_axis=0, tile...]
    gather x27 -> x0, local copies, waits for them, and re-layouts: 30.6 us -> none  [the longest x12 13.6 us: split_into_blocks(): jnp.take(products.reshape(nblocks * BLK, weights.shape[2]), slot_of_row,...]
  transfers between devices with their start and end apart: 12 -> 0, of which waited for: 8 -> 0; matrix products, arithmetic and copies ran while one was open for 6% -> 0% of each run, Pallas kernels for 0% -> 0%
where the time goes in v1:
time: 148 us
  Pallas kernels  136 us (92%)
  local copies, waits for them, and re-layouts  7.67 us (5%)
  other arithmetic  2.8 us (2%)
    pallas_call x1, Pallas kernels, fused_body(): pl.pallas_call(functools.partial(decode_kernel, n), out_shape=(jax.ShapeD...  136 us
    unnamed x3, local copies, waits for them, and re-layouts  6.34 us

profile of v1, /device:TPU:0, one launch (start us, length us, event | category | flops | bytes accessed | tf_op | source)
XLA Modules:
  0.0 147.9 jit_solution(10390545403496706352)
XLA Ops:
  1.3 0.1 fusion.3
  1.4 0.7 pad_maximum_fusion
  2.1 0.7 fusion.2.bias
  2.8 1.3 copy.14.row_adapter
  4.1 1.3 reshape.60
  5.4 3.7 %copy.15.down_hbm = bf16[8,512,192]{2,1,0:T(8,128)(2,1)} copy(bf16[8,512,192]{1,2,0:T(8,128)(2,1)} %param.17) | data formatting | bytes 3145728 | tf_op args[5]
  9.1 136.1 %shard_map.131 = (bf16[16,512]{1,0:T(8,128)(2,1)}, bf16[4,2048]{1,0:T(4,128)(2,1)}) custom-call(bf16[16,512]{1,0:T(8,128)(2,1)} %residual.1, f32[1,8192]{1,0:T(1,128)} %bitcast.14, s32[16,1]{1,0:T(8,128)} %copy.14.row_adapter, f32[4,128]{1,0:T(4,128)} %get-tuple-element.9.cosine, f32[4,128]{1,0:T(4,128)} %get-tuple-element.10.sine, f32[4,512]{1,0:T(4,128)} %fusion.2.bias, ...), custom_call_target="tpu_custom_call" | custom-call | tf_op jit(solution)/shard_map/pallas_call | solution.py:667
  145.2 1.3 copy.19
  146.5 1.3 copy.20
  (4 shorter events, 0.0 us)
